TPU v7x, 32 devices: a whole 2x2x4 slice. The times are simulated.
32 devices in a mesh: gx: 4 (over z), gy: 4 (over x, core), sa: 2 (over y).
Axes of the slice: x: 2, y: 2, z: 4, core: 2. Of those that a mesh axis runs over, the one named last changes fastest.
Arguments:
- right_side: float32 [64, 256, 256], P('gx', 'gy', 'sa'), may hold values from -8 to 8
- diagonal: float32 [64, 256, 256], P('gx', 'gy', 'sa'), may hold values from 0.25 to 2
Outputs:
- pressure: float32 [64, 256, 256], P('gx', 'gy', 'sa')
- residual: float32 [64, 256, 256], P('gx', 'gy', 'sa')
All inputs are finite; a program needn't handle non-finite values.
Results may differ from a plain program's by a relative error of at most 0.0001.
Values sent between devices are 32-bit elements; how exact they have to be, the bound alone decides.
A program may use at most 192 MiB of HBM per device.

v0:
```python
import jax
import jax.numpy as jnp
from jax import lax
from jax.sharding import PartitionSpec as P

CYCLES = 2
SWEEPS = 5
COARSE_SWEEPS = 6


damping = 2.0 / 3.0


def padded_2(cells, sides, width):
    for axis, dim in sides:
        count = lax.axis_size(axis)
        ends = count - 1
        head = lax.slice_in_dim(cells, 0, width, axis=dim)
        tail = lax.slice_in_dim(cells, cells.shape[dim] - width, cells.shape[dim], axis=dim)
        cells = jnp.concatenate(
            [
                lax.ppermute(tail, axis, [(i, (i + 1) % count) for i in range(ends)]),
                cells,
                lax.ppermute(head, axis, [((i + 1) % count, i) for i in range(ends)]),
            ],
            axis=dim,
        )
    return cells


def beside_sum(padded):
    total = padded[2:, 1:-1, 1:-1] + padded[:-2, 1:-1, 1:-1]
    total = total + padded[1:-1, 2:, 1:-1] + padded[1:-1, :-2, 1:-1]
    total = total + padded[1:-1, 1:-1, 2:] + padded[1:-1, 1:-1, :-2]
    return total


def fine_apply(field, diag_field):
    padded = padded_2(field, (("gx", 0), ("gy", 1), ("sa", 2)), 1)
    return (6.0 + diag_field) * field - beside_sum(padded)


def restrict(field):
    sx, sy, sz = field.shape
    return field.reshape(sx // 2, 2, sy // 2, 2, sz // 2, 2).sum(axis=(1, 3, 5)) * 0.5


def prolong(field):
    sx, sy, sz = field.shape
    wide = jnp.broadcast_to(field[:, None, :, None, :, None], (sx, 2, sy, 2, sz, 2))
    return wide.reshape(2 * sx, 2 * sy, 2 * sz)


def fine_smooth(source, diag_field):
    correction = damping * source / (6.0 + diag_field)
    for sweep in range(SWEEPS - 1):
        correction = correction + damping * (source - fine_apply(correction, diag_field)) / (
            6.0 + diag_field
        )
    return correction


def split_apply(field, diag_field):
    padded = padded_2(field, (("gx", 0), ("gy", 1), ("sa", 2)), 1)
    return (6.0 + diag_field) * field - beside_sum(padded)


def coarse_smooth(source, diag_field, apply_fn):
    correction = damping * source / (6.0 + diag_field)
    for sweep in range(COARSE_SWEEPS - 1):
        correction = correction + damping * (source - apply_fn(correction, diag_field)) / (
            6.0 + diag_field
        )
    return correction


def body(right_side, diagonal):
    coarse_diagonal = restrict(diagonal)
    pressure = jnp.zeros_like(right_side)
    rest = right_side
    for cycle in range(CYCLES):
        if cycle > 0:
            rest = right_side - fine_apply(pressure, diagonal)
        coarse_rest = restrict(rest)
        coarse_part = coarse_smooth(coarse_rest, coarse_diagonal, split_apply)
        fine_part = fine_smooth(rest, diagonal)
        pressure = pressure + fine_part + prolong(coarse_part)
    residual = right_side - fine_apply(pressure, diagonal)
    return (pressure, residual)


def solution(mesh):
    return jax.shard_map(
        body,
        mesh=mesh,
        in_specs=(P("gx", "gy", "sa"), P("gx", "gy", "sa")),
        out_specs=(P("gx", "gy", "sa"), P("gx", "gy", "sa")),
        check_vma=False,
    )
```

profile of v0, /device:TPU:0, one launch (start us, length us, event | category | flops | bytes accessed | tf_op | source)
XLA Modules:
  0.0 687.0 jit_solution(7476882042816037367)
XLA Ops:
  0.6 35.6 %reshape.21 = f32[8,2,32,2,64,2]{5,4,3,2,1,0:T(8,128)} reshape(f32[16,64,128]{2,1,0:T(8,128)} %param.2) | data formatting | bytes 1048576 | tf_op jit(solution)/shard_map/reshape | solution.py:45
  36.3 34.9 %reshape.22 = f32[8,2,32,2,64,2]{5,4,3,2,1,0:T(8,128)} reshape(f32[16,64,128]{2,1,0:T(8,128)S(1)} %copy-done) | data formatting | bytes 1048576 | tf_op jit(solution)/shard_map/reshape | solution.py:45
  71.2 12.3 %reduce_sum.27 = f32[8,32,64]{2,1,0:T(8,128)S(1)} reduce(f32[8,2,32,2,64,2]{5,4,3,2,1,0:T(8,128)} %reshape.21, f32[]{:T(128)} %constant.3.clone.1), dimensions={1,3,5}, to_apply=%region_0.0 | reduce | flops 114688 | bytes 589828 | tf_op jit(solution)/shard_map/reduce_sum | solution.py:45
  83.4 12.2 %reduce_sum.28 = f32[8,32,64]{2,1,0:T(8,128)S(1)} reduce(f32[8,2,32,2,64,2]{5,4,3,2,1,0:T(8,128)} %reshape.22, f32[]{:T(128)} %constant.3.clone.1), dimensions={1,3,5}, to_apply=%region_1.0 | reduce | flops 114688 | bytes 589828 | tf_op jit(solution)/shard_map/reduce_sum | solution.py:45
  97.0 5.6 collective-permute-start.25
  203.7 5.5 collective-permute-start.9
  219.0 5.2 collective-permute-start.47
  249.7 5.0 collective-permute-start.17
  257.6 5.4 collective-permute-start.51
  288.6 5.2 collective-permute-start.23
  297.3 11.4 %broadcast_in_dim.4 = f32[8,2,32,2,64,2]{5,4,3,2,1,0:T(8,128)} broadcast(f32[8,32,64]{2,1,0:T(8,128)S(1)} %fusion.152), dimensions={0,2,4} | broadcast | bytes 589824 | tf_op jit(solution)/shard_map/broadcast_in_dim | solution.py:50
  308.7 24.5 %reshape.23 = f32[16,64,128]{2,1,0:T(8,128)} reshape(f32[8,2,32,2,64,2]{5,4,3,2,1,0:T(8,128)} %broadcast_in_dim.4) | data formatting | bytes 1048576 | tf_op jit(solution)/shard_map/reshape | solution.py:51
  362.2 34.8 %reshape.24 = f32[8,2,32,2,64,2]{5,4,3,2,1,0:T(8,128)} reshape(f32[16,64,128]{2,1,0:T(8,128)S(1)} %get-tuple-element.3) | data formatting | bytes 1048576 | tf_op jit(solution)/shard_map/reshape | solution.py:45
  397.1 12.2 %reduce_sum.29 = f32[8,32,64]{2,1,0:T(8,128)S(1)} reduce(f32[8,2,32,2,64,2]{5,4,3,2,1,0:T(8,128)} %reshape.24, f32[]{:T(128)} %constant.3.clone.1), dimensions={1,3,5}, to_apply=%region_2.0 | reduce | flops 114688 | bytes 589828 | tf_op jit(solution)/shard_map/reduce_sum | solution.py:45
  410.7 4.8 collective-permute-start.85
  478.4 6.5 collective-permute-start.63
  497.2 5.1 collective-permute-start.103
  519.1 5.9 collective-permute-start.69
  536.6 5.2 collective-permute-start.107
  568.2 5.2 collective-permute-start.77
  578.0 5.4 collective-permute-start.111
  608.8 5.2 collective-permute-start.83
  619.3 11.4 %broadcast_in_dim.5 = f32[8,2,32,2,64,2]{5,4,3,2,1,0:T(8,128)} broadcast(f32[8,32,64]{2,1,0:T(8,128)S(1)} %fusion.102), dimensions={0,2,4} | broadcast | bytes 589824 | tf_op jit(solution)/shard_map/broadcast_in_dim | solution.py:50
  630.7 24.5 %reshape.25 = f32[16,64,128]{2,1,0:T(8,128)} reshape(f32[8,2,32,2,64,2]{5,4,3,2,1,0:T(8,128)} %broadcast_in_dim.5) | data formatting | bytes 1048576 | tf_op jit(solution)/shard_map/reshape | solution.py:51
  (449 shorter events, 394.5 us)
Async XLA Ops:
  182.0 15.1 %collective-permute-start.42 = (f32[1,32,64]{2,1,0:T(8,128)S(1)}, f32[1,32,64]{2,1,0:T(8,128)S(1)}, u32[]{:S(2)}, u32[]{:S(2)}) collective-permute-start(f32[1,32,64]{2,1,0:T(8,128)S(1)} %get-tuple-element.117), channel_id=1, source_target_pairs={{8,0},{16,8},{24,16},{9,1},{17,9},{25,17},{10,2},{18,10},{26,18},{... | collective-permute-start | bytes 24584 | tf_op jit(solution)/shard_map/ppermute | solution.py:24
  183.3 13.9 %collective-permute-start.43 = (f32[1,32,64]{2,1,0:T(8,128)S(1)}, f32[1,32,64]{2,1,0:T(8,128)S(1)}, u32[]{:S(2)}, u32[]{:S(2)}) collective-permute-start(f32[1,32,64]{2,1,0:T(8,128)S(1)} %get-tuple-element.116), channel_id=1, source_target_pairs={{0,8},{8,16},{16,24},{1,9},{9,17},{17,25},{2,10},{10,18},{18,26},{... | collective-permute-start | bytes 24584 | tf_op jit(solution)/shard_map/ppermute | solution.py:22
  219.0 15.8 %collective-permute-start.47 = (f32[10,34,1]{2,1,0:T(8,128)S(1)}, f32[10,34,1]{2,1,0:T(8,128)}, u32[]{:S(2)}, u32[]{:S(2)}) collective-permute-start(f32[10,34,1]{2,1,0:T(8,128)S(1)} %get-tuple-element.77), channel_id=1, source_target_pairs={{0,1},{2,3},{4,5},{6,7},{8,9},{10,11},{12,13},{14,15},{16,17},{18,... | collective-permute-start | bytes 4088 | tf_op jit(solution)/shard_map/ppermute | solution.py:22
  241.2 15.1 %collective-permute-start.48 = (f32[1,32,64]{2,1,0:T(8,128)S(1)}, f32[1,32,64]{2,1,0:T(8,128)S(1)}, u32[]{:S(2)}, u32[]{:S(2)}) collective-permute-start(f32[1,32,64]{2,1,0:T(8,128)S(1)} %get-tuple-element.115), channel_id=1, source_target_pairs={{8,0},{16,8},{24,16},{9,1},{17,9},{25,17},{10,2},{18,10},{26,18},{... | collective-permute-start | bytes 24584 | tf_op jit(solution)/shard_map/ppermute | solution.py:24
  242.5 13.8 %collective-permute-start.49 = (f32[1,32,64]{2,1,0:T(8,128)S(1)}, f32[1,32,64]{2,1,0:T(8,128)S(1)}, u32[]{:S(2)}, u32[]{:S(2)}) collective-permute-start(f32[1,32,64]{2,1,0:T(8,128)S(1)} %get-tuple-element.114), channel_id=1, source_target_pairs={{0,8},{8,16},{16,24},{1,9},{9,17},{17,25},{2,10},{10,18},{18,26},{... | collective-permute-start | bytes 24584 | tf_op jit(solution)/shard_map/ppermute | solution.py:22
  249.7 13.3 %collective-permute-start.17 = (f32[18,66,1]{1,2,0:T(1,128)S(1)}, f32[18,66,1]{1,2,0:T(1,128)S(1)}, u32[]{:S(2)}, u32[]{:S(2)}) collective-permute-start(f32[18,66,1]{1,2,0:T(1,128)S(1)} %copy.14), channel_id=1, source_target_pairs={{0,1},{2,3},{4,5},{6,7},{8,9},{10,11},{12,13},{14,15},{16,17},{18,... | collective-permute-start | bytes 14264 | tf_op jit(solution)/shard_map/ppermute | solution.py:22
  256.3 15.9 %collective-permute-start.50 = (f32[10,1,64]{2,1,0:T(1,128)S(1)}, f32[10,1,64]{2,1,0:T(1,128)S(1)}, u32[]{:S(2)}, u32[]{:S(2)}) collective-permute-start(f32[10,1,64]{2,1,0:T(1,128)S(1)} %get-tuple-element.95), channel_id=1, source_target_pairs={{2,0},{4,2},{6,4},{3,1},{5,3},{7,5},{10,8},{12,10},{14,12},{11,9},... | collective-permute-start | bytes 7688 | tf_op jit(solution)/shard_map/ppermute | solution.py:24
  257.6 14.6 %collective-permute-start.51 = (f32[10,1,64]{2,1,0:T(1,128)S(1)}, f32[10,1,64]{2,1,0:T(1,128)S(1)}, u32[]{:S(2)}, u32[]{:S(2)}) collective-permute-start(f32[10,1,64]{2,1,0:T(1,128)S(1)} %get-tuple-element.94), channel_id=1, source_target_pairs={{0,2},{2,4},{4,6},{1,3},{3,5},{5,7},{8,10},{10,12},{12,14},{9,11},... | collective-permute-start | bytes 7688 | tf_op jit(solution)/shard_map/ppermute | solution.py:22
  279.3 16.1 %collective-permute-start.53 = (f32[10,34,1]{2,1,0:T(8,128)}, f32[10,34,1]{2,1,0:T(8,128)S(1)}, u32[]{:S(2)}, u32[]{:S(2)}) collective-permute-start(f32[10,34,1]{2,1,0:T(8,128)} %get-tuple-element.75), channel_id=1, source_target_pairs={{0,1},{2,3},{4,5},{6,7},{8,9},{10,11},{12,13},{14,15},{16,17},{18,... | collective-permute-start | bytes 4088 | tf_op jit(solution)/shard_map/ppermute | solution.py:22
  288.6 44.6 %collective-permute-start.23 = (f32[18,66,1]{1,2,0:T(1,128)S(1)}, f32[18,66,1]{1,2,0:T(1,128)S(1)}, u32[]{:S(2)}, u32[]{:S(2)}) collective-permute-start(f32[18,66,1]{1,2,0:T(1,128)S(1)} %copy.18), channel_id=1, source_target_pairs={{0,1},{2,3},{4,5},{6,7},{8,9},{10,11},{12,13},{14,15},{16,17},{18,... | collective-permute-start | bytes 14264 | tf_op jit(solution)/shard_map/ppermute | solution.py:22
  294.1 39.5 %collective-permute-start.22 = (f32[18,66,1]{1,2,0:T(1,128)S(1)}, f32[18,66,1]{1,2,0:T(1,128)S(1)}, u32[]{:S(2)}, u32[]{:S(2)}) collective-permute-start(f32[18,66,1]{1,2,0:T(1,128)S(1)} %copy.16), channel_id=1, source_target_pairs={{1,0},{3,2},{5,4},{7,6},{9,8},{11,10},{13,12},{15,14},{17,16},{19,... | collective-permute-start | bytes 14264 | tf_op jit(solution)/shard_map/ppermute | solution.py:24
  488.4 14.0 %collective-permute-start.65 = (f32[18,66,1]{1,2,0:T(1,128)S(1)}, f32[18,66,1]{1,2,0:T(1,128)S(1)}, u32[]{:S(2)}, u32[]{:S(2)}) collective-permute-start(f32[18,66,1]{1,2,0:T(1,128)S(1)} %copy.26), channel_id=1, source_target_pairs={{0,1},{2,3},{4,5},{6,7},{8,9},{10,11},{12,13},{14,15},{16,17},{18,... | collective-permute-start | bytes 14264 | tf_op jit(solution)/shard_map/ppermute | solution.py:22
  496.0 16.7 %collective-permute-start.102 = (f32[1,32,64]{2,1,0:T(8,128)}, f32[1,32,64]{2,1,0:T(8,128)S(1)}, u32[]{:S(2)}, u32[]{:S(2)}) collective-permute-start(f32[1,32,64]{2,1,0:T(8,128)} %get-tuple-element.107), channel_id=1, source_target_pairs={{8,0},{16,8},{24,16},{9,1},{17,9},{25,17},{10,2},{18,10},{26,18},{... | collective-permute-start | bytes 24584 | tf_op jit(solution)/shard_map/ppermute | solution.py:24
  497.2 15.4 %collective-permute-start.103 = (f32[1,32,64]{2,1,0:T(8,128)}, f32[1,32,64]{2,1,0:T(8,128)}, u32[]{:S(2)}, u32[]{:S(2)}) collective-permute-start(f32[1,32,64]{2,1,0:T(8,128)} %get-tuple-element.106), channel_id=1, source_target_pairs={{0,8},{8,16},{16,24},{1,9},{9,17},{17,25},{2,10},{10,18},{18,26},{... | collective-permute-start | bytes 24584 | tf_op jit(solution)/shard_map/ppermute | solution.py:22
  528.6 14.6 %collective-permute-start.71 = (f32[18,66,1]{1,2,0:T(1,128)S(1)}, f32[18,66,1]{1,2,0:T(1,128)S(1)}, u32[]{:S(2)}, u32[]{:S(2)}) collective-permute-start(f32[18,66,1]{1,2,0:T(1,128)S(1)} %copy.30), channel_id=1, source_target_pairs={{0,1},{2,3},{4,5},{6,7},{8,9},{10,11},{12,13},{14,15},{16,17},{18,... | collective-permute-start | bytes 14264 | tf_op jit(solution)/shard_map/ppermute | solution.py:22
  536.6 16.8 %collective-permute-start.107 = (f32[10,34,1]{2,1,0:T(8,128)}, f32[10,34,1]{2,1,0:T(8,128)}, u32[]{:S(2)}, u32[]{:S(2)}) collective-permute-start(f32[10,34,1]{2,1,0:T(8,128)} %get-tuple-element.67), channel_id=1, source_target_pairs={{0,1},{2,3},{4,5},{6,7},{8,9},{10,11},{12,13},{14,15},{16,17},{18,... | collective-permute-start | bytes 4088 | tf_op jit(solution)/shard_map/ppermute | solution.py:22
  559.4 16.8 %collective-permute-start.108 = (f32[1,32,64]{2,1,0:T(8,128)S(1)}, f32[1,32,64]{2,1,0:T(8,128)S(1)}, u32[]{:S(2)}, u32[]{:S(2)}) collective-permute-start(f32[1,32,64]{2,1,0:T(8,128)S(1)} %get-tuple-element.105), channel_id=1, source_target_pairs={{8,0},{16,8},{24,16},{9,1},{17,9},{25,17},{10,2},{18,10},{26,18},{... | collective-permute-start | bytes 24584 | tf_op jit(solution)/shard_map/ppermute | solution.py:24
  560.7 15.5 %collective-permute-start.109 = (f32[1,32,64]{2,1,0:T(8,128)S(1)}, f32[1,32,64]{2,1,0:T(8,128)S(1)}, u32[]{:S(2)}, u32[]{:S(2)}) collective-permute-start(f32[1,32,64]{2,1,0:T(8,128)S(1)} %get-tuple-element.104), channel_id=1, source_target_pairs={{0,8},{8,16},{16,24},{1,9},{9,17},{17,25},{2,10},{10,18},{18,26},{... | collective-permute-start | bytes 24584 | tf_op jit(solution)/shard_map/ppermute | solution.py:22
  568.2 15.3 %collective-permute-start.77 = (f32[18,66,1]{1,2,0:T(1,128)S(1)}, f32[18,66,1]{1,2,0:T(1,128)S(1)}, u32[]{:S(2)}, u32[]{:S(2)}) collective-permute-start(f32[18,66,1]{1,2,0:T(1,128)S(1)} %copy.34), channel_id=1, source_target_pairs={{0,1},{2,3},{4,5},{6,7},{8,9},{10,11},{12,13},{14,15},{16,17},{18,... | collective-permute-start | bytes 14264 | tf_op jit(solution)/shard_map/ppermute | solution.py:22
  576.8 16.9 %collective-permute-start.110 = (f32[10,1,64]{2,1,0:T(1,128)}, f32[10,1,64]{2,1,0:T(1,128)S(1)}, u32[]{:S(2)}, u32[]{:S(2)}) collective-permute-start(f32[10,1,64]{2,1,0:T(1,128)} %get-tuple-element.85), channel_id=1, source_target_pairs={{2,0},{4,2},{6,4},{3,1},{5,3},{7,5},{10,8},{12,10},{14,12},{11,9},... | collective-permute-start | bytes 7688 | tf_op jit(solution)/shard_map/ppermute | solution.py:24
  578.0 15.6 %collective-permute-start.111 = (f32[10,1,64]{2,1,0:T(1,128)S(1)}, f32[10,1,64]{2,1,0:T(1,128)S(1)}, u32[]{:S(2)}, u32[]{:S(2)}) collective-permute-start(f32[10,1,64]{2,1,0:T(1,128)S(1)} %get-tuple-element.84), channel_id=1, source_target_pairs={{0,2},{2,4},{4,6},{1,3},{3,5},{5,7},{8,10},{10,12},{12,14},{9,11},... | collective-permute-start | bytes 7688 | tf_op jit(solution)/shard_map/ppermute | solution.py:22
  600.5 16.2 %collective-permute-start.113 = (f32[10,34,1]{2,1,0:T(8,128)}, f32[10,34,1]{2,1,0:T(8,128)S(1)}, u32[]{:S(2)}, u32[]{:S(2)}) collective-permute-start(f32[10,34,1]{2,1,0:T(8,128)} %get-tuple-element.65), channel_id=1, source_target_pairs={{0,1},{2,3},{4,5},{6,7},{8,9},{10,11},{12,13},{14,15},{16,17},{18,... | collective-permute-start | bytes 4088 | tf_op jit(solution)/shard_map/ppermute | solution.py:22
  608.8 46.4 %collective-permute-start.83 = (f32[18,66,1]{1,2,0:T(1,128)S(1)}, f32[18,66,1]{1,2,0:T(1,128)S(1)}, u32[]{:S(2)}, u32[]{:S(2)}) collective-permute-start(f32[18,66,1]{1,2,0:T(1,128)S(1)} %copy.38), channel_id=1, source_target_pairs={{0,1},{2,3},{4,5},{6,7},{8,9},{10,11},{12,13},{14,15},{16,17},{18,... | collective-permute-start | bytes 14264 | tf_op jit(solution)/shard_map/ppermute | solution.py:22
  615.4 41.0 %collective-permute-start.82 = (f32[18,66,1]{1,2,0:T(1,128)S(1)}, f32[18,66,1]{1,2,0:T(1,128)S(1)}, u32[]{:S(2)}, u32[]{:S(2)}) collective-permute-start(f32[18,66,1]{1,2,0:T(1,128)S(1)} %copy.36), channel_id=1, source_target_pairs={{1,0},{3,2},{5,4},{7,6},{9,8},{11,10},{13,12},{15,14},{17,16},{19,... | collective-permute-start | bytes 14264 | tf_op jit(solution)/shard_map/ppermute | solution.py:24
  (136 other events, 1600.3 us)
where the time goes:
time: 694 us; the launch traced here: 687 us
  starting transfers between devices  324 us (47%)
  local copies, waits for them, and re-layouts  231 us (33%)
  other arithmetic  68.3 us (10%)
  waiting for transfers between devices  60.6 us (9%)
    ppermute x60, starting transfers between devices, padded_2(): lax.ppermute(tail, axis, [(i, (i + 1) % count) for i in range(ends)])  247 us
    reshape x3, local copies, waits for them, and re-layouts, restrict(): field.reshape(sx // 2, 2, sy // 2, 2, sz // 2, 2).sum(axis=(1, 3, 5)) * 0.5  105 us
    ppermute x60, starting transfers between devices, padded_2(): lax.ppermute(head, axis, [((i + 1) % count, i) for i in range(ends)])  77.6 us
    reshape x2, local copies, waits for them, and re-layouts, prolong(): return wide.reshape(2 * sx, 2 * sy, 2 * sz)  48.9 us
    reduce_sum x3, other arithmetic, restrict(): field.reshape(sx // 2, 2, sy // 2, 2, sz // 2, 2).sum(axis=(1, 3, 5)) * 0.5  36.7 us
    ppermute x60, waiting for transfers between devices, padded_2(): lax.ppermute(tail, axis, [(i, (i + 1) % count) for i in range(ends)])  31.3 us
    ppermute x60, waiting for transfers between devices, padded_2(): lax.ppermute(head, axis, [((i + 1) % count, i) for i in range(ends)])  29.3 us
    broadcast_in_dim x2, local copies, waits for them, and re-layouts, prolong(): jnp.broadcast_to(field[:, None, :, None, :, None], (sx, 2, sy, 2, sz, 2))  22.8 us
  transfers between devices with their start and end apart: 120, of which 31 were waited for; matrix products, arithmetic and copies ran while one was open for 19% of the time, Pallas kernels for 0%

commit v1 on v0

v1 whole, which is shorter than its diff:
```python
import functools

import jax
import jax.numpy as jnp
from jax import lax
from jax.experimental import pallas as pl
from jax.experimental.pallas import tpu as pltpu
from jax.sharding import PartitionSpec as P

CYCLES = 2
SWEEPS = 5
COARSE_SWEEPS = 6
W = 2.0 / 3.0
AXES = ("gx", "gy", "sa")
MESH = pl.DeviceIdType.MESH
S = 8
L = 128


class Level:
    def __init__(self, nx, nj, dz, refs):
        self.nx, self.nj, self.dz = nx, nj, dz
        self.E, self.F, self.G, self.YS, self.YR, self.ZS, self.ZR, self.ssem, self.rsem = refs


def scratch_of(nx, nj):
    return [
        pltpu.VMEM((2, nx + 2, nj, S, L), jnp.float32),
        pltpu.VMEM((nx, nj, S, L), jnp.float32),
        pltpu.VMEM((nx, nj, S, L), jnp.float32),
        pltpu.VMEM((2, 2, nx, L), jnp.float32),
        pltpu.VMEM((2, 2, nx, L), jnp.float32),
        pltpu.VMEM((2, S, L), jnp.float32),
        pltpu.VMEM((2, S, L), jnp.float32),
        pltpu.SemaphoreType.DMA((2, 5)),
        pltpu.SemaphoreType.DMA((2, 5)),
    ]


def kernel(sizes, nx, nj, f_ref, d_ref, p_ref, r_ref, *scratch):
    fine = Level(nx, nj, 1, scratch[0:9])
    coarse = Level(nx // 2, nj // 2, 2, scratch[9:18])
    PB = scratch[18]
    gx, gy, sa = (lax.axis_index(a) for a in AXES)
    ngx, ngy, _ = sizes
    has = [gx > 0, gx < ngx - 1, gy > 0, gy < ngy - 1, None]
    to = [
        (gx - 1, gy, sa),
        (gx + 1, gy, sa),
        (gx, gy - 1, sa),
        (gx, gy + 1, sa),
        (gx, gy, 1 - sa),
    ]

    lane = lax.broadcasted_iota(jnp.int32, (S, L), 1)
    row = lax.broadcasted_iota(jnp.int32, (S, L), 0)
    even = lane % 2 == 0
    zero = jnp.zeros((S, L), jnp.float32)

    def when(cond, fn):
        if cond is None:
            fn()
        else:
            pl.when(cond)(fn)

    def copies(lv, slot):
        pairs = [
            (lv.E.at[slot, 1], lv.E.at[slot, lv.nx + 1]),
            (lv.E.at[slot, lv.nx], lv.E.at[slot, 0]),
            (lv.YS.at[slot, 0], lv.YR.at[slot, 1]),
            (lv.YS.at[slot, 1], lv.YR.at[slot, 0]),
            (lv.ZS.at[slot], lv.ZR.at[slot]),
        ]
        back = [1, 0, 3, 2, 4]
        return [
            pltpu.make_async_remote_copy(
                src_ref=a,
                dst_ref=b,
                send_sem=lv.ssem.at[slot, i],
                recv_sem=lv.rsem.at[slot, back[i]],
                device_id=to[i],
                device_id_type=MESH,
            )
            for i, (a, b) in enumerate(pairs)
        ]

    def arrivals(lv, slot):
        cs = copies(lv, slot)
        return [cs[1], cs[0], cs[3], cs[2], cs[4]]

    def send(lv, slot):
        cs = copies(lv, slot)
        for i in range(5):
            when(has[i], cs[i].start)

    def wait(lv, slot):
        cs = copies(lv, slot)
        ar = arrivals(lv, slot)
        for i in range(5):
            def both(i=i):
                cs[i].wait_send()
                ar[i].wait_recv()

            when(has[i], both)

    def face(lv):
        base = jnp.where(sa == 0, L - lv.dz, 0)
        return lax.rem(lane - base + L, L) // lv.dz

    def put(lv, slot, x, tiles, acc):
        rel = face(lv)
        for j, t in enumerate(tiles):
            lv.E[slot, x + 1, j] = t
            moved = t if j == 0 else pltpu.roll(t, lv.dz * j, 1)
            acc = jnp.where(rel == j, moved, acc)
        lv.YS[slot, 0, pl.ds(x, 1), :] = tiles[0][0:1]
        lv.YS[slot, 1, pl.ds(x, 1), :] = tiles[-1][S - 1 : S]
        return pltpu.roll(acc, L - lv.dz * lv.nj, 1)

    def put_end(lv, slot, acc):
        over = (lv.nx * lv.nj * lv.dz) % L
        lv.ZS[slot] = acc if over == 0 else pltpu.roll(acc, over, 1)

    def face_start(lv, slot):
        z = lv.ZR[slot]
        return jnp.where(sa == 0, pltpu.roll(z, L - lv.dz, 1), pltpu.roll(z, lv.dz, 1))

    def around(lv, slot, x, halo):
        nj, dz = lv.nj, lv.dz
        mine = face(lv) == 0
        c = [lv.E[slot, x + 1, j] for j in range(nj)]
        below = jnp.where(row == 0, lv.YR[slot, 0, pl.ds(x, 1), :], pltpu.roll(c[-1], 1, 0))
        above = jnp.where(row == S - 1, lv.YR[slot, 1, pl.ds(x, 1), :], pltpu.roll(c[0], S - 1, 0))
        ext = [below] + c + [above]
        sums = []
        for j in range(nj):
            t = lv.E[slot, x, j] + lv.E[slot, x + 2, j] + (ext[j] + ext[j + 2])
            zl = jnp.where(lane < dz, 0.0, pltpu.roll(c[j], dz, 1))
            zr = jnp.where(lane >= L - dz, 0.0, pltpu.roll(c[j], L - dz, 1))
            h = halo if j == 0 else pltpu.roll(halo, L - dz * j, 1)
            sums.append(t + (zl + zr) + jnp.where(mine, h, 0.0))
        return c, sums, pltpu.roll(halo, L - dz * nj, 1)

    def sweep(lv, src, last):
        dst = 1 - src

        def plane(x, carry):
            halo, acc = carry
            c, sums, halo = around(lv, src, x, halo)
            new = [
                (1.0 - W) * c[j] + lv.G[x, j] * (lv.F[x, j] + sums[j]) for j in range(lv.nj)
            ]
            if last:
                for j in range(lv.nj):
                    lv.E[dst, x + 1, j] = new[j]
            else:
                acc = put(lv, dst, x, new, acc)
            return halo, acc

        _, acc = lax.fori_loop(0, lv.nx, plane, (face_start(lv, src), zero))
        if not last:
            put_end(lv, dst, acc)

    def restrict(tiles):
        t = (tiles[0] + tiles[1]) + (tiles[2] + tiles[3])
        return 0.5 * (t + jnp.where(even, pltpu.roll(t, L - 1, 1), pltpu.roll(t, 1, 1)))

    def begin(slot, first):
        def plane(X, carry):
            facc, cacc = carry
            f = [[None] * nj, [None] * nj]
            d = [[None] * nj, [None] * nj]
            for i in range(2):
                x = 2 * X + i
                for j in range(nj):
                    if first:
                        f[i][j] = f_ref[x, pl.ds(j, S, stride=nj), :]
                        fine.F[x, j] = f[i][j]
                        d[i][j] = d_ref[x, pl.ds(j, S, stride=nj), :]
                        fine.G[x, j] = W / (6.0 + d[i][j])
                    else:
                        f[i][j] = fine.F[x, j]
                facc = put(
                    fine, slot, x, [fine.G[x, j] * f[i][j] for j in range(nj)], facc
                )
            new = []
            for J in range(nj // 2):
                cf = restrict([f[i][2 * J + k] for i in range(2) for k in range(2)])
                coarse.F[X, J] = cf
                if first:
                    cd = restrict([d[i][2 * J + k] for i in range(2) for k in range(2)])
                    coarse.G[X, J] = W / (6.0 + cd)
                new.append(coarse.G[X, J] * cf)
            return facc, put(coarse, slot, X, new, cacc)

        facc, cacc = lax.fori_loop(0, nx // 2, plane, (zero, zero))
        put_end(fine, slot, facc)
        put_end(coarse, slot, cacc)

    for lv in (fine, coarse):
        for slot in range(2):
            for plane in (0, lv.nx + 1):
                lv.E[slot, plane] = jnp.zeros((lv.nj, S, L), jnp.float32)
            lv.YR[slot] = jnp.zeros((2, lv.nx, L), jnp.float32)

    barrier = pltpu.get_barrier_semaphore()
    for i in range(5):
        def hello(i=i):
            pl.semaphore_signal(barrier, inc=1, device_id=to[i], device_id_type=MESH)

        when(has[i], hello)
    count = 1 + sum(h.astype(jnp.int32) for h in has[:4])
    pl.semaphore_wait(barrier, count)

    slot = 0
    for cycle in range(CYCLES):
        begin(slot, cycle == 0)
        send(fine, slot)
        send(coarse, slot)
        fs = cs = slot
        for step in range(max(SWEEPS, COARSE_SWEEPS) - 1):
            if step < SWEEPS - 1:
                last = step == SWEEPS - 2
                wait(fine, fs)
                sweep(fine, fs, last)
                fs = 1 - fs
                if not last:
                    send(fine, fs)
            if step < COARSE_SWEEPS - 1:
                last = step == COARSE_SWEEPS - 2
                wait(coarse, cs)
                sweep(coarse, cs, last)
                cs = 1 - cs
                if not last:
                    send(coarse, cs)

        def add(X, acc):
            for i in range(2):
                x = 2 * X + i
                tiles = []
                for j in range(nj):
                    t = fine.E[fs, x + 1, j] + coarse.E[cs, X + 1, j // 2]
                    if cycle > 0:
                        t = t + PB[x, j]
                    if cycle < CYCLES - 1:
                        PB[x, j] = t
                    else:
                        p_ref[x, pl.ds(j, S, stride=nj), :] = t
                    tiles.append(t)
                acc = put(fine, fs, x, tiles, acc)
            return acc

        put_end(fine, fs, lax.fori_loop(0, nx // 2, add, zero))
        send(fine, fs)
        wait(fine, fs)

        def rest(x, halo):
            c, sums, halo = around(fine, fs, x, halo)
            for j in range(nj):
                at = pl.ds(j, S, stride=nj)
                r = f_ref[x, at, :] - ((6.0 + d_ref[x, at, :]) * c[j] - sums[j])
                if cycle < CYCLES - 1:
                    fine.F[x, j] = r
                else:
                    r_ref[x, at, :] = r
            return halo

        lax.fori_loop(0, nx, rest, face_start(fine, fs))
        slot = 1 - fs


def solution(mesh):
    sizes = tuple(mesh.shape[a] for a in AXES)
    assert sizes[2] == 2

    def body(right_side, diagonal):
        nx, ny, nz = right_side.shape
        assert nz == L and ny % (2 * S) == 0 and nx % 2 == 0
        nj = ny // S
        assert nx * nj <= L
        shape = jax.ShapeDtypeStruct(right_side.shape, jnp.float32)
        vmem = pl.BlockSpec(memory_space=pltpu.VMEM)
        return pl.pallas_call(
            functools.partial(kernel, sizes, nx, nj),
            out_shape=(shape, shape),
            in_specs=[vmem, vmem],
            out_specs=(vmem, vmem),
            scratch_shapes=scratch_of(nx, nj)
            + scratch_of(nx // 2, nj // 2)
            + [pltpu.VMEM((nx, nj, S, L), jnp.float32)],
            compiler_params=pltpu.CompilerParams(
                collective_id=0, has_side_effects=True, vmem_limit_bytes=32 * 1024 * 1024
            ),
        )(right_side, diagonal)

    return jax.shard_map(
        body,
        mesh=mesh,
        in_specs=(P(*AXES), P(*AXES)),
        out_specs=(P(*AXES), P(*AXES)),
        check_vma=False,
    )
```

time: 694 us -> 86 us (0.12)
  starting transfers between devices: 324 us -> 0 us
  local copies, waits for them, and re-layouts: 231 us -> 3.66 us
  Pallas kernels: 0 us -> 81.5 us
  other arithmetic: 68.3 us -> 0 us
  waiting for transfers between devices: 60.6 us -> 0 us
    ppermute x120 -> x0, starting transfers between devices: 324 us -> none  [the longest x60 247 us: padded_2(): lax.ppermute(tail, axis, [(i, (i + 1) % count) for i in range(ends)])]
    reshape x5 -> x0, local copies, waits for them, and re-layouts: 154 us -> none  [the longest x3 105 us: restrict(): field.reshape(sx // 2, 2, sy // 2, 2, sz // 2, 2).sum(axis=(1, 3, 5)) * 0.5]
    pallas_call x0 -> x1, Pallas kernels: none -> 81.5 us  [body(): pl.pallas_call(functools.partial(kernel, sizes, nx, nj), out_shape=(shape...]
    ppermute x120 -> x0, waiting for transfers between devices: 60.6 us -> none  [the longest x60 31.3 us: padded_2(): lax.ppermute(tail, axis, [(i, (i + 1) % count) for i in range(ends)])]
    reduce_sum x3 -> x0, other arithmetic: 36.7 us -> none  [restrict(): field.reshape(sx // 2, 2, sy // 2, 2, sz // 2, 2).sum(axis=(1, 3, 5)) * 0.5]
    slice x60 -> x0, local copies, waits for them, and re-layouts: 34 us -> none  [the longest x30 20.9 us: padded_2(): head = lax.slice_in_dim(cells, 0, width, axis=dim)]
    broadcast_in_dim x2 -> x0, local copies, waits for them, and re-layouts: 22.8 us -> none  [prolong(): jnp.broadcast_to(field[:, None, :, None, :, None], (sx, 2, sy, 2, sz, 2))]
    add x18 -> x0, other arithmetic: 22.5 us -> none  [the longest x6 11.2 us: fine_smooth(): correction + damping * (source - fine_apply(correction, diag_field)) / (6...]
  transfers between devices with their start and end apart: 120 -> 0, of which waited for: 31 -> 0; matrix products, arithmetic and copies ran while one was open for 19% -> 0% of each run, Pallas kernels for 0% -> 0%
where the time goes in v1:
time: 86 us; the launch traced here: 85.8 us
  Pallas kernels  81.5 us (95%)
  local copies, waits for them, and re-layouts  3.66 us (4%)
    pallas_call x1, Pallas kernels, body(): pl.pallas_call(functools.partial(kernel, sizes, nx, nj), out_shape=(shape...  81.5 us
    unnamed x6, local copies, waits for them, and re-layouts  3.66 us

profile of v1, /device:TPU:0, one launch (start us, length us, event | category | flops | bytes accessed | tf_op | source)
XLA Modules:
  0.0 85.8 jit_solution(4853759005773266418)
XLA Ops:
  0.6 0.0 copy-start
  0.6 1.0 %copy-done = f32[16,64,128]{2,1,0:T(8,128)S(1)} copy-done((f32[16,64,128]{2,1,0:T(8,128)S(1)}, f32[16,64,128]{2,1,0:T(8,128)}, u32[]{:S(2)}) %copy-start) | copy-done | bytes 524312
  1.7 0.0 copy-start.1
  1.7 1.0 %copy-done.1 = f32[16,64,128]{2,1,0:T(8,128)S(1)} copy-done((f32[16,64,128]{2,1,0:T(8,128)S(1)}, f32[16,64,128]{2,1,0:T(8,128)}, u32[]{:S(2)}) %copy-start.1) | copy-done | bytes 524312
  2.7 81.5 %shard_map.41 = (f32[16,64,128]{2,1,0:T(8,128)S(1)}, f32[16,64,128]{2,1,0:T(8,128)S(1)}) custom-call(f32[16,64,128]{2,1,0:T(8,128)S(1)} %copy-done, f32[16,64,128]{2,1,0:T(8,128)S(1)} %copy-done.1), custom_call_target="tpu_custom_call" | custom-call | tf_op jit(solution)/shard_map/pallas_call | solution.py:283
  84.2 0.8 copy.6
  85.0 0.8 copy.7
Async XLA Ops:
  0.6 1.0 %copy-start = (f32[16,64,128]{2,1,0:T(8,128)S(1)}, f32[16,64,128]{2,1,0:T(8,128)}, u32[]{:S(2)}) copy-start(f32[16,64,128]{2,1,0:T(8,128)} %f_ref.1) | copy-start | bytes 1572868
  1.7 1.0 %copy-start.1 = (f32[16,64,128]{2,1,0:T(8,128)S(1)}, f32[16,64,128]{2,1,0:T(8,128)}, u32[]{:S(2)}) copy-start(f32[16,64,128]{2,1,0:T(8,128)} %d_ref.1) | copy-start | bytes 1572868

commit v2 on v1

--- a/solution.py
+++ b/solution.py
@@ -15,11 +15,13 @@
 MESH = pl.DeviceIdType.MESH
 S = 8
 L = 128
+UNIT = 16
 
 
 class Level:
     def __init__(self, nx, nj, dz, refs):
         self.nx, self.nj, self.dz = nx, nj, dz
+        self.unit = UNIT // dz
         self.E, self.F, self.G, self.YS, self.YR, self.ZS, self.ZR, self.ssem, self.rsem = refs
 
 
@@ -107,25 +109,40 @@
         base = jnp.where(sa == 0, L - lv.dz, 0)
         return lax.rem(lane - base + L, L) // lv.dz
 
-    def put(lv, slot, x, tiles, acc):
+    def loop(count, unit, fn, carry):
+        unit = min(unit, count)
+
+        def group(g, carry):
+            for i in range(unit):
+                carry = fn(g * unit, i, carry)
+            return carry
+
+        if unit == count:
+            return group(0, carry)
+        return lax.fori_loop(0, count // unit, group, carry)
+
+    def turn(t, by):
+        by %= L
+        return t if by == 0 else pltpu.roll(t, by, 1)
+
+    def put(lv, slot, x, i, tiles, acc):
         rel = face(lv)
         for j, t in enumerate(tiles):
             lv.E[slot, x + 1, j] = t
-            moved = t if j == 0 else pltpu.roll(t, lv.dz * j, 1)
-            acc = jnp.where(rel == j, moved, acc)
+            k = i * lv.nj + j
+            acc = jnp.where(rel == k, turn(t, lv.dz * k), acc)
         lv.YS[slot, 0, pl.ds(x, 1), :] = tiles[0][0:1]
         lv.YS[slot, 1, pl.ds(x, 1), :] = tiles[-1][S - 1 : S]
-        return pltpu.roll(acc, L - lv.dz * lv.nj, 1)
+        return turn(acc, -lv.dz * lv.nj * lv.unit) if i == lv.unit - 1 else acc
 
     def put_end(lv, slot, acc):
-        over = (lv.nx * lv.nj * lv.dz) % L
-        lv.ZS[slot] = acc if over == 0 else pltpu.roll(acc, over, 1)
+        lv.ZS[slot] = turn(acc, lv.nx * lv.nj * lv.dz)
 
     def face_start(lv, slot):
         z = lv.ZR[slot]
         return jnp.where(sa == 0, pltpu.roll(z, L - lv.dz, 1), pltpu.roll(z, lv.dz, 1))
 
-    def around(lv, slot, x, halo):
+    def around(lv, slot, x, i, halo):
         nj, dz = lv.nj, lv.dz
         mine = face(lv) == 0
         c = [lv.E[slot, x + 1, j] for j in range(nj)]
@@ -137,16 +154,19 @@
             t = lv.E[slot, x, j] + lv.E[slot, x + 2, j] + (ext[j] + ext[j + 2])
             zl = jnp.where(lane < dz, 0.0, pltpu.roll(c[j], dz, 1))
             zr = jnp.where(lane >= L - dz, 0.0, pltpu.roll(c[j], L - dz, 1))
-            h = halo if j == 0 else pltpu.roll(halo, L - dz * j, 1)
+            h = turn(halo, -dz * (i * nj + j))
             sums.append(t + (zl + zr) + jnp.where(mine, h, 0.0))
-        return c, sums, pltpu.roll(halo, L - dz * nj, 1)
+        if i == lv.unit - 1:
+            halo = turn(halo, -dz * nj * lv.unit)
+        return c, sums, halo
 
     def sweep(lv, src, last):
         dst = 1 - src
 
-        def plane(x, carry):
+        def plane(first, i, carry):
             halo, acc = carry
-            c, sums, halo = around(lv, src, x, halo)
+            x = first + i
+            c, sums, halo = around(lv, src, x, i, halo)
             new = [
                 (1.0 - W) * c[j] + lv.G[x, j] * (lv.F[x, j] + sums[j]) for j in range(lv.nj)
             ]
@@ -154,10 +174,10 @@
                 for j in range(lv.nj):
                     lv.E[dst, x + 1, j] = new[j]
             else:
-                acc = put(lv, dst, x, new, acc)
+                acc = put(lv, dst, x, i, new, acc)
             return halo, acc
 
-        _, acc = lax.fori_loop(0, lv.nx, plane, (face_start(lv, src), zero))
+        _, acc = loop(lv.nx, lv.unit, plane, (face_start(lv, src), zero))
         if not last:
             put_end(lv, dst, acc)
 
@@ -166,8 +186,9 @@
         return 0.5 * (t + jnp.where(even, pltpu.roll(t, L - 1, 1), pltpu.roll(t, 1, 1)))
 
     def begin(slot, first):
-        def plane(X, carry):
+        def plane(start, I, carry):
             facc, cacc = carry
+            X = start + I
             f = [[None] * nj, [None] * nj]
             d = [[None] * nj, [None] * nj]
             for i in range(2):
@@ -180,9 +201,8 @@
                         fine.G[x, j] = W / (6.0 + d[i][j])
                     else:
                         f[i][j] = fine.F[x, j]
-                facc = put(
-                    fine, slot, x, [fine.G[x, j] * f[i][j] for j in range(nj)], facc
-                )
+                new = [fine.G[x, j] * f[i][j] for j in range(nj)]
+                facc = put(fine, slot, x, 2 * I + i, new, facc)
             new = []
             for J in range(nj // 2):
                 cf = restrict([f[i][2 * J + k] for i in range(2) for k in range(2)])
@@ -191,9 +211,9 @@
                     cd = restrict([d[i][2 * J + k] for i in range(2) for k in range(2)])
                     coarse.G[X, J] = W / (6.0 + cd)
                 new.append(coarse.G[X, J] * cf)
-            return facc, put(coarse, slot, X, new, cacc)
-
-        facc, cacc = lax.fori_loop(0, nx // 2, plane, (zero, zero))
+            return facc, put(coarse, slot, X, I, new, cacc)
+
+        facc, cacc = loop(nx // 2, coarse.unit, plane, (zero, zero))
         put_end(fine, slot, facc)
         put_end(coarse, slot, cacc)
 
@@ -234,7 +254,8 @@
                 if not last:
                     send(coarse, cs)
 
-        def add(X, acc):
+        def add(start, I, acc):
+            X = start + I
             for i in range(2):
                 x = 2 * X + i
                 tiles = []
@@ -247,15 +268,16 @@
                     else:
                         p_ref[x, pl.ds(j, S, stride=nj), :] = t
                     tiles.append(t)
-                acc = put(fine, fs, x, tiles, acc)
+                acc = put(fine, fs, x, 2 * I + i, tiles, acc)
             return acc
 
-        put_end(fine, fs, lax.fori_loop(0, nx // 2, add, zero))
+        put_end(fine, fs, loop(nx // 2, coarse.unit, add, zero))
         send(fine, fs)
         wait(fine, fs)
 
-        def rest(x, halo):
-            c, sums, halo = around(fine, fs, x, halo)
+        def rest(first, i, halo):
+            x = first + i
+            c, sums, halo = around(fine, fs, x, i, halo)
             for j in range(nj):
                 at = pl.ds(j, S, stride=nj)
                 r = f_ref[x, at, :] - ((6.0 + d_ref[x, at, :]) * c[j] - sums[j])
@@ -265,7 +287,7 @@
                     r_ref[x, at, :] = r
             return halo
 
-        lax.fori_loop(0, nx, rest, face_start(fine, fs))
+        loop(nx, fine.unit, rest, face_start(fine, fs))
         slot = 1 - fs
 
 

time: 86 us -> 56.2 us (0.65)
  Pallas kernels: 81.5 us -> 51.7 us
    pallas_call x1, Pallas kernels: 81.5 us -> 51.7 us  [body(): pl.pallas_call(functools.partial(kernel, sizes, nx, nj), out_shape=(shape...]
where the time goes in v2:
time: 56.2 us; the launch traced here: 56 us
  Pallas kernels  51.7 us (92%)
  local copies, waits for them, and re-layouts  3.66 us (7%)
  between operations  0.65 us (1%)
    pallas_call x1, Pallas kernels, body(): pl.pallas_call(functools.partial(kernel, sizes, nx, nj), out_shape=(shape...  51.7 us
    unnamed x6, local copies, waits for them, and re-layouts  3.66 us

profile of v2, /device:TPU:0, one launch (start us, length us, event | category | flops | bytes accessed | tf_op | source)
XLA Modules:
  0.0 56.0 jit_solution(4125143380527708721)
XLA Ops:
  0.6 0.0 copy-start
  0.6 1.0 %copy-done = f32[16,64,128]{2,1,0:T(8,128)S(1)} copy-done((f32[16,64,128]{2,1,0:T(8,128)S(1)}, f32[16,64,128]{2,1,0:T(8,128)}, u32[]{:S(2)}) %copy-start) | copy-done | bytes 524312
  1.7 0.0 copy-start.1
  1.7 1.0 %copy-done.1 = f32[16,64,128]{2,1,0:T(8,128)S(1)} copy-done((f32[16,64,128]{2,1,0:T(8,128)S(1)}, f32[16,64,128]{2,1,0:T(8,128)}, u32[]{:S(2)}) %copy-start.1) | copy-done | bytes 524312
  2.7 51.7 %shard_map.41 = (f32[16,64,128]{2,1,0:T(8,128)S(1)}, f32[16,64,128]{2,1,0:T(8,128)S(1)}) custom-call(f32[16,64,128]{2,1,0:T(8,128)S(1)} %copy-done, f32[16,64,128]{2,1,0:T(8,128)S(1)} %copy-done.1), custom_call_target="tpu_custom_call" | custom-call | tf_op jit(solution)/shard_map/pallas_call | solution.py:305
  54.4 0.8 %copy.6 = f32[16,64,128]{2,1,0:T(8,128)} copy(f32[16,64,128]{2,1,0:T(8,128)S(1)} %get-tuple-element.4) | data formatting | bytes 1048576
  55.2 0.8 %copy.7 = f32[16,64,128]{2,1,0:T(8,128)} copy(f32[16,64,128]{2,1,0:T(8,128)S(1)} %get-tuple-element.5) | data formatting | bytes 1048576
Async XLA Ops:
  0.6 1.0 %copy-start = (f32[16,64,128]{2,1,0:T(8,128)S(1)}, f32[16,64,128]{2,1,0:T(8,128)}, u32[]{:S(2)}) copy-start(f32[16,64,128]{2,1,0:T(8,128)} %f_ref.1) | copy-start | bytes 1572868
  1.7 1.0 %copy-start.1 = (f32[16,64,128]{2,1,0:T(8,128)S(1)}, f32[16,64,128]{2,1,0:T(8,128)}, u32[]{:S(2)}) copy-start(f32[16,64,128]{2,1,0:T(8,128)} %d_ref.1) | copy-start | bytes 1572868

commit v3 on v2

--- a/solution.py
+++ b/solution.py
@@ -22,6 +22,7 @@
     def __init__(self, nx, nj, dz, refs):
         self.nx, self.nj, self.dz = nx, nj, dz
         self.unit = UNIT // dz
+        self.sent = [False, False]
         self.E, self.F, self.G, self.YS, self.YR, self.ZS, self.ZR, self.ssem, self.rsem = refs
 
 
@@ -39,10 +40,16 @@
     ]
 
 
-def kernel(sizes, nx, nj, f_ref, d_ref, p_ref, r_ref, *scratch):
+def kernel(sizes, nx, nj, f_hbm, d_hbm, p_ref, r_ref, *scratch):
     fine = Level(nx, nj, 1, scratch[0:9])
     coarse = Level(nx // 2, nj // 2, 2, scratch[9:18])
-    PB = scratch[18]
+    PB, f_ref, d_ref, isem = scratch[18:]
+    loads = [
+        pltpu.make_async_copy(f_hbm, f_ref, isem.at[0]),
+        pltpu.make_async_copy(d_hbm, d_ref, isem.at[1]),
+    ]
+    for load in loads:
+        load.start()
     gx, gy, sa = (lax.axis_index(a) for a in AXES)
     ngx, ngy, _ = sizes
     has = [gx > 0, gx < ngx - 1, gy > 0, gy < ngy - 1, None]
@@ -94,16 +101,20 @@
         cs = copies(lv, slot)
         for i in range(5):
             when(has[i], cs[i].start)
+        lv.sent[slot] = True
+
+    def free(lv, slot):
+        if lv.sent[slot]:
+            cs = copies(lv, slot)
+            for i in range(5):
+                when(has[i], cs[i].wait_send)
+            lv.sent[slot] = False
 
     def wait(lv, slot):
-        cs = copies(lv, slot)
         ar = arrivals(lv, slot)
         for i in range(5):
-            def both(i=i):
-                cs[i].wait_send()
-                ar[i].wait_recv()
-
-            when(has[i], both)
+            when(has[i], ar[i].wait_recv)
+        free(lv, 1 - slot)
 
     def face(lv):
         base = jnp.where(sa == 0, L - lv.dz, 0)
@@ -186,36 +197,45 @@
         return 0.5 * (t + jnp.where(even, pltpu.roll(t, L - 1, 1), pltpu.roll(t, 1, 1)))
 
     def begin(slot, first):
-        def plane(start, I, carry):
-            facc, cacc = carry
+        def low(start, I, acc):
             X = start + I
-            f = [[None] * nj, [None] * nj]
-            d = [[None] * nj, [None] * nj]
-            for i in range(2):
-                x = 2 * X + i
-                for j in range(nj):
-                    if first:
-                        f[i][j] = f_ref[x, pl.ds(j, S, stride=nj), :]
-                        fine.F[x, j] = f[i][j]
-                        d[i][j] = d_ref[x, pl.ds(j, S, stride=nj), :]
-                        fine.G[x, j] = W / (6.0 + d[i][j])
-                    else:
-                        f[i][j] = fine.F[x, j]
-                new = [fine.G[x, j] * f[i][j] for j in range(nj)]
-                facc = put(fine, slot, x, 2 * I + i, new, facc)
             new = []
             for J in range(nj // 2):
-                cf = restrict([f[i][2 * J + k] for i in range(2) for k in range(2)])
+                cells = [(2 * X + i, 2 * J + k) for i in range(2) for k in range(2)]
+                if first:
+                    at = [(x, pl.ds(j, S, stride=nj)) for x, j in cells]
+                    cf = restrict([f_ref[x, y, :] for x, y in at])
+                    cd = restrict([d_ref[x, y, :] for x, y in at])
+                    coarse.G[X, J] = W / (6.0 + cd)
+                else:
+                    cf = restrict([fine.F[x, j] for x, j in cells])
                 coarse.F[X, J] = cf
+                new.append(coarse.G[X, J] * cf)
+            return put(coarse, slot, X, I, new, acc)
+
+        put_end(coarse, slot, loop(nx // 2, coarse.unit, low, zero))
+        if first:
+            pl.semaphore_wait(barrier, count)
+        send(coarse, slot)
+
+        def high(start, i, acc):
+            x = start + i
+            new = []
+            for j in range(nj):
                 if first:
-                    cd = restrict([d[i][2 * J + k] for i in range(2) for k in range(2)])
-                    coarse.G[X, J] = W / (6.0 + cd)
-                new.append(coarse.G[X, J] * cf)
-            return facc, put(coarse, slot, X, I, new, cacc)
-
-        facc, cacc = loop(nx // 2, coarse.unit, plane, (zero, zero))
-        put_end(fine, slot, facc)
-        put_end(coarse, slot, cacc)
+                    y = pl.ds(j, S, stride=nj)
+                    f = f_ref[x, y, :]
+                    g = W / (6.0 + d_ref[x, y, :])
+                    fine.F[x, j] = f
+                    fine.G[x, j] = g
+                else:
+                    f = fine.F[x, j]
+                    g = fine.G[x, j]
+                new.append(g * f)
+            return put(fine, slot, x, i, new, acc)
+
+        put_end(fine, slot, loop(nx, fine.unit, high, zero))
+        send(fine, slot)
 
     for lv in (fine, coarse):
         for slot in range(2):
@@ -230,15 +250,21 @@
 
         when(has[i], hello)
     count = 1 + sum(h.astype(jnp.int32) for h in has[:4])
-    pl.semaphore_wait(barrier, count)
+    for load in loads:
+        load.wait()
 
     slot = 0
     for cycle in range(CYCLES):
         begin(slot, cycle == 0)
-        send(fine, slot)
-        send(coarse, slot)
         fs = cs = slot
         for step in range(max(SWEEPS, COARSE_SWEEPS) - 1):
+            if step < COARSE_SWEEPS - 1:
+                last = step == COARSE_SWEEPS - 2
+                wait(coarse, cs)
+                sweep(coarse, cs, last)
+                cs = 1 - cs
+                if not last:
+                    send(coarse, cs)
             if step < SWEEPS - 1:
                 last = step == SWEEPS - 2
                 wait(fine, fs)
@@ -246,13 +272,6 @@
                 fs = 1 - fs
                 if not last:
                     send(fine, fs)
-            if step < COARSE_SWEEPS - 1:
-                last = step == COARSE_SWEEPS - 2
-                wait(coarse, cs)
-                sweep(coarse, cs, last)
-                cs = 1 - cs
-                if not last:
-                    send(coarse, cs)
 
         def add(start, I, acc):
             X = start + I
@@ -289,6 +308,11 @@
 
         loop(nx, fine.unit, rest, face_start(fine, fs))
         slot = 1 - fs
+        free(fine, slot)
+        free(coarse, slot)
+    for lv in (fine, coarse):
+        for at in range(2):
+            free(lv, at)
 
 
 def solution(mesh):
@@ -302,14 +326,20 @@
         assert nx * nj <= L
         shape = jax.ShapeDtypeStruct(right_side.shape, jnp.float32)
         vmem = pl.BlockSpec(memory_space=pltpu.VMEM)
+        hbm = pl.BlockSpec(memory_space=pltpu.HBM)
         return pl.pallas_call(
             functools.partial(kernel, sizes, nx, nj),
             out_shape=(shape, shape),
-            in_specs=[vmem, vmem],
+            in_specs=[hbm, hbm],
             out_specs=(vmem, vmem),
             scratch_shapes=scratch_of(nx, nj)
             + scratch_of(nx // 2, nj // 2)
-            + [pltpu.VMEM((nx, nj, S, L), jnp.float32)],
+            + [
+                pltpu.VMEM((nx, nj, S, L), jnp.float32),
+                pltpu.VMEM(right_side.shape, jnp.float32),
+                pltpu.VMEM(right_side.shape, jnp.float32),
+                pltpu.SemaphoreType.DMA((2,)),
+            ],
             compiler_params=pltpu.CompilerParams(
                 collective_id=0, has_side_effects=True, vmem_limit_bytes=32 * 1024 * 1024
             ),

time: 56.2 us -> 50 us (0.89)
  Pallas kernels: 51.7 us -> 45.5 us
    pallas_call x1, Pallas kernels: 51.7 us -> 45.5 us  [body(): pl.pallas_call(functools.partial(kernel, sizes, nx, nj), out_shape=(shape...]
where the time goes in v3:
time: 50 us; the launch traced here: 49.8 us
  Pallas kernels  45.5 us (91%)
  local copies, waits for them, and re-layouts  3.66 us (7%)
  between operations  0.65 us (1%)
    pallas_call x1, Pallas kernels, body(): pl.pallas_call(functools.partial(kernel, sizes, nx, nj), out_shape=(shape...  45.5 us
    unnamed x6, local copies, waits for them, and re-layouts  3.66 us

profile of v3, /device:TPU:0, one launch (start us, length us, event | category | flops | bytes accessed | tf_op | source)
XLA Modules:
  0.0 49.8 jit_solution(16627471117176347572)
XLA Ops:
  0.6 0.0 copy-start
  0.6 1.0 %copy-done = f32[16,64,128]{2,1,0:T(8,128)S(1)} copy-done((f32[16,64,128]{2,1,0:T(8,128)S(1)}, f32[16,64,128]{2,1,0:T(8,128)}, u32[]{:S(2)}) %copy-start) | copy-done | bytes 524312
  1.7 0.0 copy-start.1
  1.7 1.0 %copy-done.1 = f32[16,64,128]{2,1,0:T(8,128)S(1)} copy-done((f32[16,64,128]{2,1,0:T(8,128)S(1)}, f32[16,64,128]{2,1,0:T(8,128)}, u32[]{:S(2)}) %copy-start.1) | copy-done | bytes 524312
  2.7 45.5 %shard_map.41 = (f32[16,64,128]{2,1,0:T(8,128)S(1)}, f32[16,64,128]{2,1,0:T(8,128)S(1)}) custom-call(f32[16,64,128]{2,1,0:T(8,128)S(1)} %copy-done, f32[16,64,128]{2,1,0:T(8,128)S(1)} %copy-done.1), custom_call_target="tpu_custom_call" | custom-call | tf_op jit(solution)/shard_map/pallas_call | solution.py:330
  48.2 0.8 %copy.6 = f32[16,64,128]{2,1,0:T(8,128)} copy(f32[16,64,128]{2,1,0:T(8,128)S(1)} %get-tuple-element.4) | data formatting | bytes 1048576
  49.0 0.8 %copy.7 = f32[16,64,128]{2,1,0:T(8,128)} copy(f32[16,64,128]{2,1,0:T(8,128)S(1)} %get-tuple-element.5) | data formatting | bytes 1048576
Async XLA Ops:
  0.6 1.0 %copy-start = (f32[16,64,128]{2,1,0:T(8,128)S(1)}, f32[16,64,128]{2,1,0:T(8,128)}, u32[]{:S(2)}) copy-start(f32[16,64,128]{2,1,0:T(8,128)} %f_hbm.1) | copy-start | bytes 1572868
  1.7 1.0 %copy-start.1 = (f32[16,64,128]{2,1,0:T(8,128)S(1)}, f32[16,64,128]{2,1,0:T(8,128)}, u32[]{:S(2)}) copy-start(f32[16,64,128]{2,1,0:T(8,128)} %d_hbm.1) | copy-start | bytes 1572868

commit v4 on v3

--- a/solution.py
+++ b/solution.py
@@ -97,9 +97,9 @@
         cs = copies(lv, slot)
         return [cs[1], cs[0], cs[3], cs[2], cs[4]]
 
-    def send(lv, slot):
+    def send(lv, slot, dirs=(2, 3, 4)):
         cs = copies(lv, slot)
-        for i in range(5):
+        for i in dirs:
             when(has[i], cs[i].start)
         lv.sent[slot] = True
 
@@ -120,7 +120,7 @@
         base = jnp.where(sa == 0, L - lv.dz, 0)
         return lax.rem(lane - base + L, L) // lv.dz
 
-    def loop(count, unit, fn, carry):
+    def loop(count, unit, fn, carry, early=None):
         unit = min(unit, count)
 
         def group(g, carry):
@@ -129,7 +129,12 @@
             return carry
 
         if unit == count:
-            return group(0, carry)
+            for n, i in enumerate([0, count - 1, *range(1, count - 1)]):
+                carry = fn(0, i, carry)
+                if n == 1 and early is not None:
+                    early()
+            return carry
+        assert early is None
         return lax.fori_loop(0, count // unit, group, carry)
 
     def turn(t, by):
@@ -144,10 +149,10 @@
             acc = jnp.where(rel == k, turn(t, lv.dz * k), acc)
         lv.YS[slot, 0, pl.ds(x, 1), :] = tiles[0][0:1]
         lv.YS[slot, 1, pl.ds(x, 1), :] = tiles[-1][S - 1 : S]
-        return turn(acc, -lv.dz * lv.nj * lv.unit) if i == lv.unit - 1 else acc
+        return turn(acc, -lv.dz * lv.nj * lv.unit) if i == lv.unit - 1 < lv.nx - 1 else acc
 
     def put_end(lv, slot, acc):
-        lv.ZS[slot] = turn(acc, lv.nx * lv.nj * lv.dz)
+        lv.ZS[slot] = turn(acc, lv.nx * lv.nj * lv.dz if lv.unit < lv.nx else 0)
 
     def face_start(lv, slot):
         z = lv.ZR[slot]
@@ -167,7 +172,7 @@
             zr = jnp.where(lane >= L - dz, 0.0, pltpu.roll(c[j], L - dz, 1))
             h = turn(halo, -dz * (i * nj + j))
             sums.append(t + (zl + zr) + jnp.where(mine, h, 0.0))
-        if i == lv.unit - 1:
+        if i == lv.unit - 1 < lv.nx - 1:
             halo = turn(halo, -dz * nj * lv.unit)
         return c, sums, halo
 
@@ -188,7 +193,8 @@
                 acc = put(lv, dst, x, i, new, acc)
             return halo, acc
 
-        _, acc = loop(lv.nx, lv.unit, plane, (face_start(lv, src), zero))
+        early = None if last else lambda: send(lv, dst, (0, 1))
+        _, acc = loop(lv.nx, lv.unit, plane, (face_start(lv, src), zero), early)
         if not last:
             put_end(lv, dst, acc)
 
@@ -216,7 +222,7 @@
         put_end(coarse, slot, loop(nx // 2, coarse.unit, low, zero))
         if first:
             pl.semaphore_wait(barrier, count)
-        send(coarse, slot)
+        send(coarse, slot, range(5))
 
         def high(start, i, acc):
             x = start + i
@@ -235,7 +241,7 @@
             return put(fine, slot, x, i, new, acc)
 
         put_end(fine, slot, loop(nx, fine.unit, high, zero))
-        send(fine, slot)
+        send(fine, slot, range(5))
 
     for lv in (fine, coarse):
         for slot in range(2):
@@ -290,7 +296,7 @@
                 acc = put(fine, fs, x, 2 * I + i, tiles, acc)
             return acc
 
-        put_end(fine, fs, loop(nx // 2, coarse.unit, add, zero))
+        put_end(fine, fs, loop(nx // 2, coarse.unit, add, zero, lambda: send(fine, fs, (0, 1))))
         send(fine, fs)
         wait(fine, fs)
 

time: 50 us -> 47.1 us (0.942)
  Pallas kernels: 45.5 us -> 42.6 us
    pallas_call x1, Pallas kernels: 45.5 us -> 42.6 us  [body(): pl.pallas_call(functools.partial(kernel, sizes, nx, nj), out_shape=(shape...]
where the time goes in v4:
time: 47.1 us; the launch traced here: 46.9 us
  Pallas kernels  42.6 us (90%)
  local copies, waits for them, and re-layouts  3.66 us (8%)
  between operations  0.65 us (1%)
    pallas_call x1, Pallas kernels, body(): pl.pallas_call(functools.partial(kernel, sizes, nx, nj), out_shape=(shape...  42.6 us
    unnamed x6, local copies, waits for them, and re-layouts  3.66 us

profile of v4, /device:TPU:0, one launch (start us, length us, event | category | flops | bytes accessed | tf_op | source)
XLA Modules:
  0.0 46.9 jit_solution(12697754773323490362)
XLA Ops:
  0.6 0.0 copy-start
  0.6 1.0 %copy-done = f32[16,64,128]{2,1,0:T(8,128)S(1)} copy-done((f32[16,64,128]{2,1,0:T(8,128)S(1)}, f32[16,64,128]{2,1,0:T(8,128)}, u32[]{:S(2)}) %copy-start) | copy-done | bytes 524312
  1.7 0.0 copy-start.1
  1.7 1.0 %copy-done.1 = f32[16,64,128]{2,1,0:T(8,128)S(1)} copy-done((f32[16,64,128]{2,1,0:T(8,128)S(1)}, f32[16,64,128]{2,1,0:T(8,128)}, u32[]{:S(2)}) %copy-start.1) | copy-done | bytes 524312
  2.7 42.6 %shard_map.41 = (f32[16,64,128]{2,1,0:T(8,128)S(1)}, f32[16,64,128]{2,1,0:T(8,128)S(1)}) custom-call(f32[16,64,128]{2,1,0:T(8,128)S(1)} %copy-done, f32[16,64,128]{2,1,0:T(8,128)S(1)} %copy-done.1), custom_call_target="tpu_custom_call" | custom-call | tf_op jit(solution)/shard_map/pallas_call | solution.py:336
  45.3 0.8 %copy.6 = f32[16,64,128]{2,1,0:T(8,128)} copy(f32[16,64,128]{2,1,0:T(8,128)S(1)} %get-tuple-element.4) | data formatting | bytes 1048576
  46.1 0.8 %copy.7 = f32[16,64,128]{2,1,0:T(8,128)} copy(f32[16,64,128]{2,1,0:T(8,128)S(1)} %get-tuple-element.5) | data formatting | bytes 1048576
Async XLA Ops:
  0.6 1.0 %copy-start = (f32[16,64,128]{2,1,0:T(8,128)S(1)}, f32[16,64,128]{2,1,0:T(8,128)}, u32[]{:S(2)}) copy-start(f32[16,64,128]{2,1,0:T(8,128)} %f_hbm.1) | copy-start | bytes 1572868
  1.7 1.0 %copy-start.1 = (f32[16,64,128]{2,1,0:T(8,128)S(1)}, f32[16,64,128]{2,1,0:T(8,128)}, u32[]{:S(2)}) copy-start(f32[16,64,128]{2,1,0:T(8,128)} %d_hbm.1) | copy-start | bytes 1572868
